TPU v7x, 256 devices: a whole 4x4x8 slice. The times are simulated.
256 devices in a mesh: gx: 4 (over y), gy: 8 (over x, z_hi), gz: 8 (over z_lo, core).
Axes of the slice: x: 4, y: 4, z: 8 (z_hi: 2, z_lo: 4; z = z_hi * 4 + z_lo), core: 2. Of those that a mesh axis runs over, the one named last changes fastest.
Arguments:
- charges: float32 [262144], P(('gx', 'gy', 'gz')), may hold values from -6 to 6
- mesh_start: int32 [3, 262144], P(None, ('gx', 'gy', 'gz')), may hold values from 0 to 319, as said below
- mesh_frac: float32 [3, 262144], P(None, ('gx', 'gy', 'gz')), may hold values from 0 to 1
- influence: float32 [320, 320, 320], P(('gx', 'gz'), 'gy'), may hold values from 4 to 400, as said below
Outputs:
- potential: float32 [262144], P(('gx', 'gy', 'gz'))
- forces: float32 [3, 262144], P(None, ('gx', 'gy', 'gz'))
Inputs may be any that keep to these rules, and one draw needn't show every extreme that they name: `mesh_start`: A device at position p along gx+gz (joined in that order) and position q along gy holds sites whose start along x lies in p * 10 to p * 10 + 9 and whose start along y lies in q * 40 to q * 40 + 39; starts along z take any value. influence[kz, kx, ky] equals influence[(-kz) mod 320, (-kx) mod 320, (-ky) mod 320].
All inputs are finite; a program needn't handle non-finite values.
Results may differ from a plain program's by a relative error of at most 0.00017.
Values sent between devices are 32-bit elements; how exact they have to be, the bound alone decides.
No kernel may reach another device: no remote copies, remote signals or barrier semaphores. Data moves between devices by JAX's collectives and lax.ppermute only.
A program may use at most 128 MiB of HBM per device.

v0:
```python
import functools
import math

import jax
import jax.numpy as jnp
import ml_dtypes
import numpy as np
from jax import lax
from jax.experimental import pallas as pl
from jax.experimental.pallas import tpu as pltpu
from jax.sharding import PartitionSpec as P

M = 320
PX = 10
PY = 40
GX, GY, GZ = 4, 8, 8
PENCILS = GX * GZ
SLOTS = 6
CHUNK = 8
HALF = CHUNK // 2
ROWS = GX * GY * GZ * CHUNK
GROUPS_Y = 6
STEP_Y = 8
LANES = 128
WIDE = HALF * LANES
CELLS = GROUPS_Y * PX * STEP_Y
DEEP = 1024
STRIDE = 40
PLANE_ROWS = 104
BF16 = jnp.bfloat16
F32 = jnp.float32
NT = (((1,), (1,)), ((), ()))


def halves(table):
    high = table.astype(ml_dtypes.bfloat16)
    low = (table - high.astype(np.float64)).astype(ml_dtypes.bfloat16)
    return high, low


def left_table(table):
    high, low = halves(table)
    return np.concatenate([high, high, low], axis=1)


def angles(rows, columns, period):
    phase = np.mod(np.outer(rows, columns), period)
    return phase * (2.0 * math.pi / period)


def complex_left(angle):
    c, s = np.cos(angle), np.sin(angle)
    return np.block([[c, s], [-s, c]])


def lanes_complex(angle, live):
    c, s = np.cos(angle) * live, np.sin(angle) * live
    return np.block([[c, -s], [s, c]])


def lanes_x_table():
    slot = np.arange(LANES) // STEP_Y
    y = np.arange(LANES) % STEP_Y
    live = (slot < PX)[:, None] & (y[:, None] == y[None, :]) & (slot < 10)[None, :]
    return lanes_complex(angles(slot, slot, 10), live)


def lanes_y_table():
    lane = np.arange(LANES)
    live = (lane[:, None] // 8 == lane[None, :] // 8) & (lane < 80)[:, None]
    return lanes_complex(angles(lane % 8, lane % 8, 8), live)


def wave_slots():
    waves = np.zeros((GX, SLOTS, GZ), np.int64)
    fold = np.zeros((GX, SLOTS, GZ))
    for gx in range(GX):
        for gz in range(GZ):
            p = gx * GZ + gz
            upper = p >= PENCILS // 2
            for j in range(SLOTS):
                wave = 10 * p + j
                if (j < 5 and not upper) or (j > 0 and upper) or wave == M // 2:
                    waves[gx, j, gz] = wave
                    fold[gx, j, gz] = 1.0 if wave in (0, M // 2) else 2.0
    return waves.reshape(-1), fold.reshape(-1)


@functools.lru_cache(maxsize=None)
def tables():
    waves, fold = wave_slots()
    angle = angles(waves, np.arange(M), M)
    live = (fold > 0)[:, None]
    front = np.concatenate([np.cos(angle) * live, -np.sin(angle) * live])
    scale = fold[:, None] / float(M * M * M)
    back = np.concatenate([np.cos(angle) * scale, -np.sin(angle) * scale]).T
    back = np.pad(back, [(0, 384 - M), (0, 0)])
    left_x = complex_left(angles(np.arange(32), np.arange(32), 32))
    order = np.concatenate([5 * np.arange(GY) + g for g in range(5)])
    left_y = complex_left(angles(np.arange(40), order, 40))
    lanes_x = lanes_x_table()
    lanes_y = lanes_y_table()
    lane = np.arange(LANES)
    turn_x = angles(np.arange(32), np.arange(WIDE) // STEP_Y % PX, M)
    turn_y = angles(np.arange(40), lane % 8, M)
    parts = [part for table in (lanes_x, lanes_y) for part in halves(table)]
    for table in (left_x, left_x.T, left_y, left_y.T):
        left = left_table(table)
        parts.append(np.pad(left, [(0, 0), (0, 256 - left.shape[1])]))
    turns = [np.cos(turn_x), -np.sin(turn_x), np.cos(turn_y), -np.sin(turn_y)]
    turns = [part[:, i : i + LANES] for part in turns for i in range(0, part.shape[1], LANES)]
    return dict(
        front=left_table(front),
        back=left_table(back),
        mixes=np.concatenate(parts, axis=0),
        turns=np.concatenate(turns, axis=0).astype(np.float32),
    )


def split(value):
    high = value.astype(BF16)
    low = (value - high.astype(F32)).astype(BF16)
    return high, low


def split_rows(value):
    high, low = split(value)
    return jnp.concatenate([high, low, high], axis=0)


def split_lanes(value):
    high, low = split(value)
    return jnp.concatenate([high, low, high], axis=1)


def dot(left, right):
    return jnp.dot(left, right, preferred_element_type=F32)


def dot_nt(left, right):
    return lax.dot_general(left, right, NT, preferred_element_type=F32)


def dot_lanes(form, value, high_table, low_table):
    high, low = split(value)
    return form(high, high_table) + form(low, high_table) + form(high, low_table)


def spline_weights(fraction):
    values = [1.0 - fraction, fraction] + [jnp.zeros_like(fraction) for unused in range(4)]
    for order in range(3, 6):
        factor = 1.0 / (order - 1)
        values[order - 1] = factor * fraction * values[order - 2]
        for offset in range(1, order - 1):
            values[order - offset - 1] = factor * (
                (fraction + offset) * values[order - offset - 2]
                + (order - offset - fraction) * values[order - offset - 1]
            )
        values[0] = factor * (1.0 - fraction) * values[0]
    slopes = [-values[0]] + [values[offset - 1] - values[offset] for offset in range(1, 6)]
    factor = 1.0 / 5.0
    values[5] = factor * fraction * values[4]
    for offset in range(1, 5):
        values[5 - offset] = factor * (
            (fraction + offset) * values[4 - offset] + (6 - offset - fraction) * values[5 - offset]
        )
    values[0] = factor * (1.0 - fraction) * values[0]
    return values, slopes


def place(coefficients, dimension, offset):
    result = jnp.zeros(offset.shape, F32)
    for j in range(6):
        result = jnp.where(offset == j, coefficients[j][dimension : dimension + 1], result)
    return result


def rows_below(start, length):
    return lax.broadcasted_iota(jnp.int32, (length, start.shape[1]), 0) - start


def parameters(site_ref):
    whole = site_ref[4:7].astype(jnp.int32)
    return site_ref[0:1], site_ref[1:4], whole[0:1], whole[1:2], whole[2:3]


def z_offset_short(start, first, length):
    offset = lax.broadcasted_iota(jnp.int16, (length, start.shape[1]), 0) + jnp.int16(first) - start
    return jnp.where(offset < 0, offset + jnp.int16(M), offset)


def place_split(halved, offset):
    results = [jnp.zeros(offset.shape, BF16) for unused in range(2)]
    for j in range(6):
        here = offset == j
        results = [jnp.where(here, halved[j][i], results[i]) for i in range(2)]
    return results


def pack_kernel(
    charge_in, start_in, frac_in, influence_in, out_ref, planes_ref, charge_ref, start_ref, frac_ref, slab_ref, sems
):
    copies = [
        pltpu.make_async_copy(start_in, start_ref, sems.at[0]),
        pltpu.make_async_copy(frac_in, frac_ref, sems.at[1]),
        pltpu.make_async_copy(charge_in, charge_ref, sems.at[2]),
        pltpu.make_async_copy(influence_in.at[0:SLOTS], slab_ref, sems.at[3]),
    ]
    for copy in copies:
        copy.start()
    for copy in copies[:3]:
        copy.wait()
    out_ref[0:1] = charge_ref[...]
    out_ref[1:4] = frac_ref[...]
    out_ref[4:5] = lax.rem(start_ref[0:1], PX).astype(F32)
    out_ref[5:6] = lax.rem(start_ref[1:2], PY).astype(F32)
    out_ref[6:7] = start_ref[2:3].astype(F32)
    out_ref[7:8] = jnp.zeros(charge_ref.shape, F32)
    copies[3].wait()
    half = PY // 2
    for j in range(SLOTS):
        first = j * PLANE_ROWS
        tail = slab_ref[j, :, 2 * LANES : M]
        planes_ref[first : first + PY] = slab_ref[j, :, :LANES]
        planes_ref[first + PY : first + 2 * PY] = slab_ref[j, :, LANES : 2 * LANES]
        planes_ref[first + 2 * PY : first + 2 * PY + half] = jnp.concatenate([tail[:half], tail[half:]], axis=1)
        planes_ref[first + 2 * PY + half : first + PLANE_ROWS] = jnp.zeros((PLANE_ROWS - 2 * PY - half, LANES), F32)
    planes_ref[SLOTS * PLANE_ROWS :] = jnp.zeros(((GY - SLOTS) * PLANE_ROWS, LANES), F32)


def finish_kernel(own_ref, edge_ref, inner_ref, potential_ref, forces_ref):
    total = inner_ref[...] + edge_ref[...]
    potential_ref[...] = total[0:1]
    forces_ref[...] = -own_ref[0:1] * total[1:4]


def spread_kernel(own_ref, near_ref, front_ref, out_ref, wz_ref, plane_ref):
    sites = own_ref.shape[1]
    mesh = None
    for source in range(2):
        charge, fraction, start_x, start_y, start_z = parameters((own_ref, near_ref)[source])
        values, unused = spline_weights(fraction)
        weight_x = place(values, 0, rows_below(start_x - source * PX, 16)) * charge
        weight_y = place(values, 1, rows_below(start_y, GROUPS_Y * STEP_Y))
        for part in range(0, sites, 256):
            picked = slice(part, part + 256)
            lanes = slice(source * sites + part, source * sites + part + 256)
            halved = [split(value[2:3, picked]) for value in values]
            short_z = start_z[:, picked].astype(jnp.int16)
            for block in range(0, M, 16):
                high, low = place_split(halved, z_offset_short(short_z, block, 16))
                wz_ref[0, block : block + 16, lanes] = high
                wz_ref[1, block : block + 16, lanes] = low
            for cell in range(0, WIDE, 16):
                pair = []
                for first in (cell, cell + STEP_Y):
                    if first < CELLS:
                        g, x = first // (PX * STEP_Y), first // STEP_Y % PX
                        near = weight_y[g * STEP_Y : (g + 1) * STEP_Y, picked]
                        pair.append(near * jnp.broadcast_to(weight_x[x : x + 1, picked], near.shape))
                    else:
                        pair.append(jnp.zeros((STEP_Y, 256), F32))
                high, low = split(jnp.concatenate(pair, axis=0))
                plane_ref[0, cell : cell + 16, lanes] = high
                plane_ref[1, cell : cell + 16, lanes] = low
            for i, j in ((0, 0), (0, 1), (1, 0)):
                term = dot_nt(wz_ref[i, :, lanes], plane_ref[j, :, lanes])
                mesh = term if mesh is None else mesh + term
    waves = dot(front_ref[...], split_rows(mesh))
    span = SLOTS * GZ
    for gx in range(GX):
        first = gx * GY * GZ * CHUNK
        for part in range(2):
            rows = waves[(part * GX + gx) * span : (part * GX + gx + 1) * span]
            for r in range(HALF):
                out_ref[pl.ds(first + part * HALF + r, span, stride=CHUNK), :] = rows[:, r * LANES : (r + 1) * LANES]
        out_ref[first + span * CHUNK : first + GY * GZ * CHUNK] = jnp.zeros(((GY * GZ - span) * CHUNK, LANES), F32)


def turn(real, imag, cos, sin):
    return real * cos - imag * sin, real * sin + imag * cos


def plane_kernel(in_ref, influence_ref, mixes_ref, turns_ref, out_ref, real_ref, imag_ref, real_back_ref, imag_back_ref):
    def lanes_x_table(group):
        shift = group * PX * STEP_Y % LANES
        pieces = []
        for first in range(0, 512, LANES):
            if shift:
                pieces.append(mixes_ref[first + LANES - shift : first + LANES])
            pieces.append(mixes_ref[first : first + LANES - shift])
        table = jnp.concatenate(pieces, axis=0)
        return table[:256], table[256:]

    lanes_y_table = mixes_ref[512:768], mixes_ref[768:1024]
    first = 1024
    left_x, left_xh = mixes_ref[first : first + 64, :192], mixes_ref[first + 64 : first + 128, :192]
    left_y, left_yh = mixes_ref[first + 128 : first + 208, :240], mixes_ref[first + 208 : first + 288, :240]
    cos_x, sin_x = [
        jnp.concatenate([turns_ref[(i * HALF + r) * 32 : (i * HALF + r + 1) * 32] for r in range(HALF)], axis=1)
        for i in range(2)
    ]
    cos_y, sin_y = turns_ref[256:296], turns_ref[296:336]

    def lane(value, k):
        return value[:, k * LANES : (k + 1) * LANES]

    def chunk_rows(gx, q, part, r):
        return pl.ds((gx * GY + q) * GZ * CHUNK + part * HALF + r, GZ, stride=CHUNK)

    turned = []
    for q in range(GY):
        rows = [
            jnp.concatenate([in_ref[chunk_rows(gx, q, part, r), :] for r in range(HALF)], axis=1)
            for part in range(2)
            for gx in range(GX)
        ]
        mixed = dot(left_x, split_rows(jnp.concatenate(rows, axis=0)))
        turned.append(turn(mixed[:32], mixed[32:], cos_x, sin_x))
    lanes = lax.broadcasted_iota(jnp.int32, (1, 2 * LANES), 1) % LANES

    def placed(group, rows):
        first = group * PX * STEP_Y
        row = first // LANES
        if first % LANES + PX * STEP_Y <= LANES:
            return rows[row]
        return jnp.where(lanes >= first % LANES, rows[row], rows[row + 1])

    rows = [
        jnp.concatenate([jnp.concatenate([lane(re, r), lane(im, r)], axis=1) for re, im in turned], axis=0)
        for r in range(HALF)
    ]
    groups = [
        dot_lanes(dot, placed(g, rows), *lanes_x_table(g)) for g in range(GROUPS_Y)
    ]
    spill = groups[5]
    groups[0] = groups[0] + jnp.concatenate([spill[7 * 32 :], spill[: 7 * 32]], axis=0)
    for g in range(5):
        for q in range(GY):
            first = (g * GY + q) * STRIDE
            real_ref[first : first + 32] = lane(groups[g][q * 32 : (q + 1) * 32], 0)
            imag_ref[first : first + 32] = lane(groups[g][q * 32 : (q + 1) * 32], 1)

    batch = 32
    for k in range(0, 32, batch):
        picks = [pl.ds(k + i, 40, stride=STRIDE) for i in range(batch)]
        real = jnp.concatenate([real_ref[pick, :] for pick in picks], axis=1)
        imag = jnp.concatenate([imag_ref[pick, :] for pick in picks], axis=1)
        mixed = dot(left_y, split_rows(jnp.concatenate([real, imag], axis=0)))
        turned = [
            jnp.concatenate(turn(lane(mixed[:40], i), lane(mixed[40:], i), cos_y, sin_y), axis=1)
            for i in range(batch)
        ]
        spectrum = dot_lanes(dot, jnp.concatenate(turned, axis=0), *lanes_y_table)
        influence = influence_ref[k * 40 : (k + batch) * 40]
        spectrum = spectrum * jnp.concatenate([influence, influence], axis=1)
        back = dot_lanes(dot_nt, spectrum, *lanes_y_table)
        pieces = [
            turn(lane(back[i * 40 : (i + 1) * 40], 0), lane(back[i * 40 : (i + 1) * 40], 1), cos_y, -sin_y)
            for i in range(batch)
        ]
        stacked = jnp.concatenate(
            [jnp.concatenate([piece[part] for piece in pieces], axis=1) for part in range(2)], axis=0
        )
        inverse = dot(left_yh, split_rows(stacked))
        for i in range(batch):
            real_back_ref[picks[i], :] = lane(inverse[:40], i)
            imag_back_ref[picks[i], :] = lane(inverse[40:], i)

    groups = [
        jnp.concatenate(
            [
                jnp.concatenate(
                    [ref[(g * GY + q) * STRIDE : (g * GY + q) * STRIDE + 32] for q in range(GY)], axis=0
                )
                for ref in (real_back_ref, imag_back_ref)
            ],
            axis=1,
        )
        for g in range(5)
    ]
    groups.append(jnp.concatenate([groups[0][32:], groups[0][:32]], axis=0))
    pieces = [None] * HALF
    for g in range(GROUPS_Y):
        back = dot_lanes(dot_nt, groups[g], *lanes_x_table(g))
        first = g * PX * STEP_Y
        row = first // LANES
        pieces[row] = back if pieces[row] is None else jnp.where(lanes >= first % LANES, back, pieces[row])
        if first % LANES + PX * STEP_Y > LANES:
            pieces[row + 1] = back
    for q in range(GY):
        picked = [back[q * 32 : (q + 1) * 32] for back in pieces]
        real = jnp.concatenate([lane(back, 0) for back in picked], axis=1)
        imag = jnp.concatenate([lane(back, 1) for back in picked], axis=1)
        stacked = jnp.concatenate(turn(real, imag, cos_x, -sin_x), axis=0)
        inverse = dot(left_xh, split_rows(stacked))
        for part in range(2):
            for gx in range(GX):
                tile = inverse[(part * GX + gx) * GZ : (part * GX + gx + 1) * GZ]
                for r in range(HALF):
                    out_ref[chunk_rows(gx, q, part, r), :] = lane(tile, r)


def gather_sites(site_ref, shift, columns, mesh, wz_ref, finish):
    sites = site_ref.shape[1]
    unused, fraction, start_x, start_y, start_z = parameters(site_ref)
    values, slopes = spline_weights(fraction)
    offset_x = rows_below(start_x - shift, 16)
    offset_y = rows_below(start_y, GROUPS_Y * STEP_Y)
    weight_x, slope_x = place(values, 0, offset_x), place(slopes, 0, offset_x)
    weight_y, slope_y = place(values, 1, offset_y), place(slopes, 1, offset_y)
    short_z = start_z.astype(jnp.int16)
    halved = [[split(value[2:3]) for value in coefficients] for coefficients in (values, slopes)]
    for block in range(0, M, 16):
        offset = z_offset_short(short_z, block, 16)
        for kind in range(2):
            high, low = place_split(halved[kind], offset)
            for term, part in enumerate((high, high, low)):
                row = term * 256 + block if block < 256 else 768 + term * 64 + block - 256
                wz_ref[kind, row : row + 16] = part
    for kind in range(2):
        wz_ref[kind, 960:DEEP] = jnp.zeros((64, sites), BF16)
    width = 256
    for first in range(0, sites, width):
        lanes = slice(first, first + width)
        near = dot(mesh, wz_ref[0, :, lanes])
        near_slope = dot(mesh, wz_ref[1, :, lanes])
        sums = [jnp.zeros((STEP_Y, width), F32) for unused in range(4)]
        for g in range(GROUPS_Y):
            wy = weight_y[g * STEP_Y : (g + 1) * STEP_Y, lanes]
            sy = slope_y[g * STEP_Y : (g + 1) * STEP_Y, lanes]
            for x in range(columns):
                row = (g * columns + x) * STEP_Y
                value = near[row : row + STEP_Y]
                weighted = wy * value
                wx = weight_x[x : x + 1, lanes]
                sums[0] = sums[0] + wx * weighted
                sums[1] = sums[1] + slope_x[x : x + 1, lanes] * weighted
                sums[2] = sums[2] + wx * (sy * value)
                sums[3] = sums[3] + wx * (wy * near_slope[row : row + STEP_Y])
        finish(lanes, [jnp.sum(part, axis=0, keepdims=True) for part in sums])


def deep_lanes(mesh):
    high, low = split(mesh)
    tail = jnp.concatenate([high[:, 256:M], low[:, 256:M], high[:, 256:M], jnp.zeros((mesh.shape[0], 64), BF16)], axis=1)
    return jnp.concatenate([high[:, :256], low[:, :256], high[:, :256], tail], axis=1)


def near_kernel(in_ref, near_ref, back_ref, mesh_ref, part_ref, wz_ref):
    span = SLOTS * GZ
    rows = [
        jnp.concatenate(
            [in_ref[pl.ds(gx * GY * GZ * CHUNK + part * HALF + r, span, stride=CHUNK), :] for r in range(HALF)],
            axis=1,
        )
        for part in range(2)
        for gx in range(GX)
    ]
    mesh = dot(back_ref[...], split_rows(jnp.concatenate(rows, axis=0)))
    mesh = jnp.transpose(mesh)[:CELLS]
    mesh_ref[...] = deep_lanes(mesh)
    edge = [mesh[g * PX * STEP_Y : g * PX * STEP_Y + 5 * STEP_Y] for g in range(GROUPS_Y)]
    edge = deep_lanes(jnp.concatenate(edge, axis=0))

    def finish(lanes, totals):
        for i in range(4):
            part_ref[i : i + 1, lanes] = totals[i]

    gather_sites(near_ref, PX, 5, edge, wz_ref, finish)


def own_kernel(mesh_ref, own_ref, part_ref, wz_ref):
    def finish(lanes, totals):
        for i in range(4):
            part_ref[i : i + 1, lanes] = totals[i]

    gather_sites(own_ref, 0, PX, mesh_ref[...], wz_ref, finish)


PLANE_SCRATCH = [pltpu.VMEM((40 * STRIDE, LANES), F32) for unused in range(4)]
LIMIT = pltpu.CompilerParams(vmem_limit_bytes=24 * 1024 * 1024)


def exchange(chunks):
    flat = chunks.reshape(GX * GY * GZ, 1, CHUNK * LANES)
    return lax.all_to_all(flat, ("gx", "gy", "gz"), 0, 0, tiled=True).reshape(ROWS, LANES)


def influence_along_x(planes):
    groups = [[2 * x + half for x in range(4)] for half in range(2)]
    flat = planes.reshape(GY // 2, 1, 2 * PLANE_ROWS * LANES)
    planes = lax.all_to_all(flat, "gy", 0, 0, tiled=True, axis_index_groups=groups)
    return planes.reshape(GY // 2, 2, PLANE_ROWS, LANES)


def widen_kernel(in_ref, out_ref):
    out_ref[:, :80] = in_ref[...]
    out_ref[:, 80:] = jnp.zeros((1280, LANES - 80), F32)


def influence_layout(planes):
    half = lax.axis_index("gy") % 2
    kept = lax.dynamic_index_in_dim(planes, half, 1, keepdims=False)
    sent = lax.dynamic_index_in_dim(planes, 1 - half, 1, keepdims=False)
    other = lax.ppermute(sent, "gy", [(s, s ^ 1) for s in range(SLOTS)])
    pair = [jnp.where(half == 0, kept, other), jnp.where(half == 0, other, kept)]
    planes = jnp.stack(pair, axis=1).reshape(GY, PLANE_ROWS, LANES)
    tail = planes[:, 2 * PY : 2 * PY + PY // 2]
    tail = jnp.concatenate([tail[:, :, : LANES // 2], tail[:, :, LANES // 2 :]], axis=1)
    planes = jnp.concatenate([planes[:, :PY], planes[:, PY : 2 * PY], tail], axis=2)
    planes = planes.reshape(10, 32, 8, 40).transpose(1, 3, 0, 2).reshape(1280, 80)
    return pl.pallas_call(
        widen_kernel,
        out_shape=jax.ShapeDtypeStruct((1280, LANES), F32),
        compiler_params=LIMIT,
        cost_estimate=pl.CostEstimate(flops=100000000000, bytes_accessed=1000000, transcendentals=0),
        name="widen",
    )(planes)


def body(charges, mesh_start, mesh_frac, influence):
    table = {name: jnp.asarray(value) for name, value in tables().items()}
    sites = charges.shape[0]
    own, planes = pl.pallas_call(
        pack_kernel,
        out_shape=(
            jax.ShapeDtypeStruct((8, sites), F32),
            jax.ShapeDtypeStruct((GY * PLANE_ROWS, LANES), F32),
        ),
        in_specs=[pl.BlockSpec(memory_space=pl.ANY)] * 4,
        scratch_shapes=[
            pltpu.VMEM((1, sites), F32),
            pltpu.VMEM((3, sites), jnp.int32),
            pltpu.VMEM((3, sites), F32),
            pltpu.VMEM((SLOTS, PY, M), F32),
            pltpu.SemaphoreType.DMA((4,)),
        ],
        compiler_params=pltpu.CompilerParams(vmem_limit_bytes=60 * 1024 * 1024),
        name="pack",
    )(charges.reshape(1, sites), mesh_start, mesh_frac, influence)
    near = lax.ppermute(own, ("gx", "gz"), [(p, (p + 1) % PENCILS) for p in range(PENCILS)])
    planes = influence_along_x(planes)
    chunks = pl.pallas_call(
        spread_kernel,
        out_shape=jax.ShapeDtypeStruct((ROWS, LANES), F32),
        scratch_shapes=[pltpu.VMEM((2, M, 2 * sites), BF16), pltpu.VMEM((2, WIDE, 2 * sites), BF16)],
        compiler_params=LIMIT,
        cost_estimate=pl.CostEstimate(flops=40000000000, bytes_accessed=10000000, transcendentals=0),
        name="spread",
    )(own, near, table["front"])
    planes, chunks = lax.optimization_barrier((planes, chunks))
    planes = influence_layout(planes)
    chunks = exchange(chunks)
    chunks = pl.pallas_call(
        plane_kernel,
        out_shape=jax.ShapeDtypeStruct((ROWS, LANES), F32),
        scratch_shapes=PLANE_SCRATCH,
        compiler_params=LIMIT,
        name="plane",
    )(
        chunks,
        planes,
        table["mixes"],
        table["turns"],
    )
    chunks = exchange(chunks)
    mesh, edge = pl.pallas_call(
        near_kernel,
        out_shape=(jax.ShapeDtypeStruct((CELLS, DEEP), BF16), jax.ShapeDtypeStruct((4, sites), F32)),
        scratch_shapes=[pltpu.VMEM((2, DEEP, sites), BF16)],
        compiler_params=LIMIT,
        name="near",
    )(chunks, near, table["back"])
    edge = lax.ppermute(edge, ("gx", "gz"), [(p, (p - 1) % PENCILS) for p in range(PENCILS)])
    inner = pl.pallas_call(
        own_kernel,
        out_shape=jax.ShapeDtypeStruct((4, sites), F32),
        scratch_shapes=[pltpu.VMEM((2, DEEP, sites), BF16)],
        compiler_params=LIMIT,
        name="own",
    )(mesh, own)
    potential, forces = pl.pallas_call(
        finish_kernel,
        out_shape=(jax.ShapeDtypeStruct((1, sites), F32), jax.ShapeDtypeStruct((3, sites), F32)),
        compiler_params=LIMIT,
        name="finish",
    )(own, edge, inner)
    return potential.reshape(sites), forces


def solution(mesh):
    return jax.shard_map(
        body,
        mesh=mesh,
        in_specs=(
            P(("gx", "gy", "gz")),
            P(None, ("gx", "gy", "gz")),
            P(None, ("gx", "gy", "gz")),
            P(("gx", "gz"), "gy", None),
        ),
        out_specs=(P(("gx", "gy", "gz")), P(None, ("gx", "gy", "gz"))),
        check_vma=False,
    )
```

profile of v0, /device:TPU:1, one launch (start us, length us, event | category | flops | bytes accessed | tf_op | source)
XLA Modules:
  0.0 116.5 jit_solution(7120546660964242356)
XLA Ops:
  0.6 0.0 copy-start.5
  0.6 2.0 %pack.1 = (f32[8,1024]{1,0:T(8,128)}, f32[832,128]{1,0:T(8,128)}) custom-call(f32[1,1024]{1,0:T(1,128)} %bitcast.38, s32[3,1024]{1,0:T(4,128)} %start_in.1, f32[3,1024]{1,0:T(4,128)} %frac_in.1, f32[10,40,320]{2,1,0:T(8,128)} %influence_in.1), custom_call_target="tpu_custom_call" | custom-call | tf_op jit(solution)/shard_map/pack/pallas_call | solution.py:525
  2.7 3.1 %collective-permute-start = (f32[8,1024]{1,0:T(8,128)}, f32[8,1024]{1,0:T(8,128)S(1)}, u32[]{:S(2)}, u32[]{:S(2)}) collective-permute-start(f32[8,1024]{1,0:T(8,128)} %get-tuple-element.10.own_ref), channel_id=1, source_target_pairs={{0,1},{1,2},{2,3},{3,4},{4,5},{5,6},{6,7},{7,64},{64,65},{65,66},{... | collective-permute-start | bytes 98312 | tf_op jit(solution)/shard_map/ppermute | solution.py:542
  5.8 4.0 %all-to-all-start = ((f32[4,1,26624]{2,1,0:T(1,128)}), f32[4,1,26624]{2,1,0:T(1,128)S(1)}, u32[]{:S(2)}, u32[]{:S(2)}) async-start(f32[4,1,26624]{2,1,0:T(1,128)} %bitcast.37), calls=%async_computation | async-start | bytes 851968 | tf_op jit(solution)/shard_map/all_to_all | solution.py:493
  9.8 0.0 collective-permute-done.near_ref
  9.8 0.0 copy-done.5
  9.8 0.0 copy-start.3
  9.8 0.7 copy-done.3
  10.5 4.3 %spread.1 = f32[2048,128]{1,0:T(8,128)} custom-call(f32[8,1024]{1,0:T(8,128)S(1)} %copy-done.3, f32[8,1024]{1,0:T(8,128)S(1)} %collective-permute-done.near_ref, bf16[384,960]{1,0:T(8,128)(2,1)S(1)} %copy-done.5), custom_call_target="tpu_custom_call" | custom-call | flops 40000000000 | bytes 10000000 | tf_op jit(solution)/shard_map/spread/pallas_call | solution.py:544
  14.8 3.8 %all-to-all-done = f32[4,1,26624]{2,1,0:T(1,128)S(1)} async-done(((f32[4,1,26624]{2,1,0:T(1,128)}), f32[4,1,26624]{2,1,0:T(1,128)S(1)}, u32[]{:S(2)}, u32[]{:S(2)}) %all-to-all-start) | async-done | bytes 426016 | tf_op jit(solution)/shard_map/all_to_all | solution.py:493
  18.7 7.9 %collective-permute-start.1 = (f32[4,104,128]{2,1,0:T(8,128)S(1)}, f32[4,104,128]{2,1,0:T(8,128)S(1)}, u32[]{:S(2)}, u32[]{:S(2)}) collective-permute-start(f32[4,104,128]{2,1,0:T(8,128)S(1)} %dynamic-slice_bitcast_fusion), channel_id=1, source_target_pairs={{0,8},{8,0},{16,24},{24,16},{32,40},{40,32},{1,9},{9,1},{17,25},{2... | collective-permute-start | bytes 638984 | tf_op jit(solution)/shard_map/ppermute | solution.py:506
  26.6 7.0 %all-to-all-start.1 = ((f32[256,1,1024]{2,1,0:T(1,128)}), f32[256,1,1024]{2,1,0:T(1,128)S(1)}, u32[]{:S(2)}, u32[]{:S(2)}) async-start(f32[256,1,1024]{2,1,0:T(1,128)} %bitcast.3), calls=%async_computation.1 | async-start | bytes 2097152 | tf_op jit(solution)/shard_map/all_to_all | solution.py:487
  33.6 0.0 collective-permute-done.1
  33.7 0.1 fusion.3
  33.9 0.5 reshape.43
  34.4 1.3 %copy.20 = f32[32,40,10,8]{1,0,3,2:T(8,128)} copy(f32[32,40,10,8]{1,3,0,2:T(8,128)S(1)} %bitcast.32) | data formatting | bytes 819200 | tf_op jit(solution)/shard_map/transpose | solution.py:512
  35.7 2.0 %reshape.44 = f32[1280,80]{0,1:T(8,128)S(1)} reshape(f32[32,40,10,8]{1,0,3,2:T(8,128)} %copy.20) | data formatting | bytes 819200 | tf_op jit(solution)/shard_map/reshape | solution.py:512
  37.7 0.2 copy.21.in_ref
  38.0 0.0 copy-start.1
  38.0 0.0 copy-start.2
  38.0 0.1 widen.1.influence_ref
  38.1 28.0 %all-to-all-done.1 = f32[256,1,1024]{2,1,0:T(1,128)S(1)} async-done(((f32[256,1,1024]{2,1,0:T(1,128)}), f32[256,1,1024]{2,1,0:T(1,128)S(1)}, u32[]{:S(2)}, u32[]{:S(2)}) %all-to-all-start.1) | async-done | bytes 1048608 | tf_op jit(solution)/shard_map/all_to_all | solution.py:487
  66.1 0.0 copy-done.1
  66.1 0.0 copy-done.2
  66.1 5.3 %plane.1 = f32[2048,128]{1,0:T(8,128)S(1)} custom-call(f32[2048,128]{1,0:T(8,128)S(1)} %bitcast.29, f32[1280,128]{1,0:T(8,128)S(1)} %widen.1.influence_ref, bf16[1312,256]{1,0:T(8,128)(2,1)S(1)} %copy-done.1, f32[336,128]{1,0:T(8,128)S(1)} %copy-done.2), custom_call_target="tpu_custom_call" | custom-call | tf_op jit(solution)/shard_map/plane/pallas_call | solution.py:555
  71.4 0.0 copy-start
  71.4 38.5 %all_to_all.15 = f32[256,1,1024]{2,1,0:T(1,128)S(1)} all-to-all(f32[256,1,1024]{2,1,0:T(1,128)S(1)} %bitcast.30), channel_id=1, replica_groups=mesh['gx'=4,'gy'=8,'gz'=8] {'gx','gy','gz'}, dimensions={0} | all-to-all | bytes 2097152 | tf_op jit(solution)/shard_map/all_to_all | solution.py:487
  109.9 0.0 copy-start.4
  109.9 0.0 copy-done
  109.9 2.8 %near.1 = (bf16[480,1024]{1,0:T(8,128)(2,1)S(1)}, f32[4,1024]{1,0:T(4,128)S(1)}) custom-call(f32[2048,128]{1,0:T(8,128)S(1)} %bitcast.31, f32[8,1024]{1,0:T(8,128)S(1)} %collective-permute-done.near_ref, bf16[384,1152]{1,0:T(8,128)(2,1)S(1)} %copy-done), custom_call_target="tpu_custom_call" | custom-call | tf_op jit(solution)/shard_map/near/pallas_call | solution.py:568
  112.6 0.1 collective-permute-start.2
  112.7 0.0 copy-done.4
  112.8 2.6 %own.1.inner_ref = f32[4,1024]{1,0:T(4,128)S(1)} custom-call(bf16[480,1024]{1,0:T(8,128)(2,1)S(1)} %get-tuple-element.15.mesh_ref, f32[8,1024]{1,0:T(8,128)S(1)} %copy-done.4), custom_call_target="tpu_custom_call" | custom-call | tf_op jit(solution)/shard_map/own/pallas_call | solution.py:576
  115.4 0.5 collective-permute-done.2.edge_ref
  115.9 0.6 finish.1
  (5 shorter events, 0.1 us)
Async XLA Ops:
  0.6 9.1 %copy-start.5 = (bf16[384,960]{1,0:T(8,128)(2,1)S(1)}, bf16[384,960]{1,0:T(8,128)(2,1)}, u32[]{:S(2)}) copy-start(bf16[384,960]{1,0:T(8,128)(2,1)} %constant.36.clone.front_ref) | copy-start | bytes 2211844
  2.7 7.1 %collective-permute-start = (f32[8,1024]{1,0:T(8,128)}, f32[8,1024]{1,0:T(8,128)S(1)}, u32[]{:S(2)}, u32[]{:S(2)}) collective-permute-start(f32[8,1024]{1,0:T(8,128)} %get-tuple-element.10.own_ref), channel_id=1, source_target_pairs={{0,1},{1,2},{2,3},{3,4},{4,5},{5,6},{6,7},{7,64},{64,65},{65,66},{... | collective-permute-start | bytes 98312 | tf_op jit(solution)/shard_map/ppermute | solution.py:542
  5.8 12.9 %all-to-all-start = ((f32[4,1,26624]{2,1,0:T(1,128)}), f32[4,1,26624]{2,1,0:T(1,128)S(1)}, u32[]{:S(2)}, u32[]{:S(2)}) async-start(f32[4,1,26624]{2,1,0:T(1,128)} %bitcast.37), calls=%async_computation | async-start | bytes 851968 | tf_op jit(solution)/shard_map/all_to_all | solution.py:493
  9.8 0.8 copy-start.3
  18.7 15.0 %collective-permute-start.1 = (f32[4,104,128]{2,1,0:T(8,128)S(1)}, f32[4,104,128]{2,1,0:T(8,128)S(1)}, u32[]{:S(2)}, u32[]{:S(2)}) collective-permute-start(f32[4,104,128]{2,1,0:T(8,128)S(1)} %dynamic-slice_bitcast_fusion), channel_id=1, source_target_pairs={{0,8},{8,0},{16,24},{24,16},{32,40},{40,32},{1,9},{9,1},{17,25},{2... | collective-permute-start | bytes 638984 | tf_op jit(solution)/shard_map/ppermute | solution.py:506
  26.6 39.5 %all-to-all-start.1 = ((f32[256,1,1024]{2,1,0:T(1,128)}), f32[256,1,1024]{2,1,0:T(1,128)S(1)}, u32[]{:S(2)}, u32[]{:S(2)}) async-start(f32[256,1,1024]{2,1,0:T(1,128)} %bitcast.3), calls=%async_computation.1 | async-start | bytes 2097152 | tf_op jit(solution)/shard_map/all_to_all | solution.py:487
  38.0 28.1 %copy-start.1 = (bf16[1312,256]{1,0:T(8,128)(2,1)S(1)}, bf16[1312,256]{1,0:T(8,128)(2,1)}, u32[]{:S(2)}) copy-start(bf16[1312,256]{1,0:T(8,128)(2,1)} %constant.38.clone.mixes_ref) | copy-start | bytes 2015236
  38.0 28.1 %copy-start.2 = (f32[336,128]{1,0:T(8,128)S(1)}, f32[336,128]{1,0:T(8,128)}, u32[]{:S(2)}) copy-start(f32[336,128]{1,0:T(8,128)} %constant.39.clone.turns_ref) | copy-start | bytes 516100
  71.4 38.5 %copy-start = (bf16[384,1152]{1,0:T(8,128)(2,1)S(1)}, bf16[384,1152]{1,0:T(8,128)(2,1)}, u32[]{:S(2)}) copy-start(bf16[384,1152]{1,0:T(8,128)(2,1)} %constant.37.clone.back_ref) | copy-start | bytes 2654212
  109.9 2.9 %copy-start.4 = (f32[8,1024]{1,0:T(8,128)S(1)}, f32[8,1024]{1,0:T(8,128)}, u32[]{:S(2)}) copy-start(f32[8,1024]{1,0:T(8,128)} %get-tuple-element.10.own_ref) | copy-start | bytes 98308
  112.6 3.2 %collective-permute-start.2 = (f32[4,1024]{1,0:T(4,128)S(1)}, f32[4,1024]{1,0:T(4,128)S(1)}, u32[]{:S(2)}, u32[]{:S(2)}) collective-permute-start(f32[4,1024]{1,0:T(4,128)S(1)} %get-tuple-element.14), channel_id=1, source_target_pairs={{0,199},{1,0},{2,1},{3,2},{4,3},{5,4},{6,5},{7,6},{64,7},{65,64},{... | collective-permute-start | bytes 49160 | tf_op jit(solution)/shard_map/ppermute | solution.py:575
where the time goes:
time: 117 us
  blocking collectives  38.5 us (33%)
  waiting for transfers between devices  32.3 us (28%)
  starting transfers between devices  22.1 us (19%)
  Pallas kernels  17.6 us (15%)
  local copies, waits for them, and re-layouts  4.96 us (4%)
    all_to_all x1, blocking collectives, exchange(): lax.all_to_all(flat, ('gx', 'gy', 'gz'), 0, 0, tiled=True)  38.5 us
    all_to_all x1, waiting for transfers between devices, exchange(): lax.all_to_all(flat, ('gx', 'gy', 'gz'), 0, 0, tiled=True)  28 us
    ppermute x1, starting transfers between devices, influence_layout(): other = lax.ppermute(sent, 'gy', [(s, s ^ 1) for s in range(SLOTS)])  7.9 us
    all_to_all x1, starting transfers between devices, exchange(): lax.all_to_all(flat, ('gx', 'gy', 'gz'), 0, 0, tiled=True)  7.05 us
    pallas_call x1, Pallas kernels, body(): pl.pallas_call(plane_kernel, out_shape=jax.ShapeDtypeStruct((ROWS, LANES)...  5.27 us
    pallas_call x1, Pallas kernels, body(): pl.pallas_call(spread_kernel, out_shape=jax.ShapeDtypeStruct((ROWS, LANES...  4.28 us
    all_to_all x1, starting transfers between devices, influence_along_x(): lax.all_to_all(flat, 'gy', 0, 0, tiled=True, axis_index_groups=groups)  4.01 us
    all_to_all x1, waiting for transfers between devices, influence_along_x(): lax.all_to_all(flat, 'gy', 0, 0, tiled=True, axis_index_groups=groups)  3.81 us
  transfers between devices with their start and end apart: 5, of which 3 were waited for; matrix products, arithmetic and copies ran while one was open for 4% of the time, Pallas kernels for 6%

commit v1 on v0

--- a/solution.py
+++ b/solution.py
@@ -27,6 +27,7 @@
 DEEP = 1024
 STRIDE = 40
 PLANE_ROWS = 104
+SCALE_Y = 239.0
 BF16 = jnp.bfloat16
 F32 = jnp.float32
 NT = (((1,), (1,)), ((), ()))
@@ -92,7 +93,7 @@
     angle = angles(waves, np.arange(M), M)
     live = (fold > 0)[:, None]
     front = np.concatenate([np.cos(angle) * live, -np.sin(angle) * live])
-    scale = fold[:, None] / float(M * M * M)
+    scale = fold[:, None] / (float(M * M * M) * SCALE_Y**2)
     back = np.concatenate([np.cos(angle) * scale, -np.sin(angle) * scale]).T
     back = np.pad(back, [(0, 384 - M), (0, 0)])
     left_x = complex_left(angles(np.arange(32), np.arange(32), 32))
@@ -103,7 +104,8 @@
     lane = np.arange(LANES)
     turn_x = angles(np.arange(32), np.arange(WIDE) // STEP_Y % PX, M)
     turn_y = angles(np.arange(40), lane % 8, M)
-    parts = [part for table in (lanes_x, lanes_y) for part in halves(table)]
+    parts = [part for table in (lanes_x,) for part in halves(table)]
+    parts.append(np.round(SCALE_Y * lanes_y).astype(ml_dtypes.bfloat16))
     for table in (left_x, left_x.T, left_y, left_y.T):
         left = left_table(table)
         parts.append(np.pad(left, [(0, 0), (0, 256 - left.shape[1])]))
@@ -144,6 +146,11 @@
 def dot_lanes(form, value, high_table, low_table):
     high, low = split(value)
     return form(high, high_table) + form(low, high_table) + form(high, low_table)
+
+
+def dot_exact(form, value, table):
+    high, low = split(value)
+    return form(high, table) + form(low, table)
 
 
 def spline_weights(fraction):
@@ -292,8 +299,8 @@
         table = jnp.concatenate(pieces, axis=0)
         return table[:256], table[256:]
 
-    lanes_y_table = mixes_ref[512:768], mixes_ref[768:1024]
-    first = 1024
+    lanes_y_table = mixes_ref[512:768]
+    first = 768
     left_x, left_xh = mixes_ref[first : first + 64, :192], mixes_ref[first + 64 : first + 128, :192]
     left_y, left_yh = mixes_ref[first + 128 : first + 208, :240], mixes_ref[first + 208 : first + 288, :240]
     cos_x, sin_x = [
@@ -351,10 +358,10 @@
             jnp.concatenate(turn(lane(mixed[:40], i), lane(mixed[40:], i), cos_y, sin_y), axis=1)
             for i in range(batch)
         ]
-        spectrum = dot_lanes(dot, jnp.concatenate(turned, axis=0), *lanes_y_table)
+        spectrum = dot_exact(dot, jnp.concatenate(turned, axis=0), lanes_y_table)
         influence = influence_ref[k * 40 : (k + batch) * 40]
         spectrum = spectrum * jnp.concatenate([influence, influence], axis=1)
-        back = dot_lanes(dot_nt, spectrum, *lanes_y_table)
+        back = dot_exact(dot_nt, spectrum, lanes_y_table)
         pieces = [
             turn(lane(back[i * 40 : (i + 1) * 40], 0), lane(back[i * 40 : (i + 1) * 40], 1), cos_y, -sin_y)
             for i in range(batch)

time: 117 us -> 116 us (level)
  no operation moved by 1% of the time
where the time goes in v1:
time: 116 us
  blocking collectives  38.5 us (33%)
  waiting for transfers between devices  32.3 us (28%)
  starting transfers between devices  22.1 us (19%)
  Pallas kernels  17 us (15%)
  local copies, waits for them, and re-layouts  4.96 us (4%)
    all_to_all x1, blocking collectives, exchange(): lax.all_to_all(flat, ('gx', 'gy', 'gz'), 0, 0, tiled=True)  38.5 us
    all_to_all x1, waiting for transfers between devices, exchange(): lax.all_to_all(flat, ('gx', 'gy', 'gz'), 0, 0, tiled=True)  28 us
    ppermute x1, starting transfers between devices, influence_layout(): other = lax.ppermute(sent, 'gy', [(s, s ^ 1) for s in range(SLOTS)])  7.9 us
    all_to_all x1, starting transfers between devices, exchange(): lax.all_to_all(flat, ('gx', 'gy', 'gz'), 0, 0, tiled=True)  7.05 us
    pallas_call x1, Pallas kernels, body(): pl.pallas_call(plane_kernel, out_shape=jax.ShapeDtypeStruct((ROWS, LANES)...  4.59 us
    pallas_call x1, Pallas kernels, body(): pl.pallas_call(spread_kernel, out_shape=jax.ShapeDtypeStruct((ROWS, LANES...  4.28 us
    all_to_all x1, starting transfers between devices, influence_along_x(): lax.all_to_all(flat, 'gy', 0, 0, tiled=True, axis_index_groups=groups)  4.01 us
    all_to_all x1, waiting for transfers between devices, influence_along_x(): lax.all_to_all(flat, 'gy', 0, 0, tiled=True, axis_index_groups=groups)  3.81 us
  transfers between devices with their start and end apart: 5, of which 3 were waited for; matrix products, arithmetic and copies ran while one was open for 4% of the time, Pallas kernels for 6%

profile of v1, /device:TPU:1, one launch (start us, length us, event | category | flops | bytes accessed | tf_op | source)
XLA Modules:
  0.0 115.8 jit_solution(15106387826710492079)
XLA Ops:
  0.6 0.0 copy-start.5
  0.6 2.0 %pack.1 = (f32[8,1024]{1,0:T(8,128)}, f32[832,128]{1,0:T(8,128)}) custom-call(f32[1,1024]{1,0:T(1,128)} %bitcast.38, s32[3,1024]{1,0:T(4,128)} %start_in.1, f32[3,1024]{1,0:T(4,128)} %frac_in.1, f32[10,40,320]{2,1,0:T(8,128)} %influence_in.1), custom_call_target="tpu_custom_call" | custom-call | tf_op jit(solution)/shard_map/pack/pallas_call | solution.py:532
  2.7 3.1 %collective-permute-start = (f32[8,1024]{1,0:T(8,128)}, f32[8,1024]{1,0:T(8,128)S(1)}, u32[]{:S(2)}, u32[]{:S(2)}) collective-permute-start(f32[8,1024]{1,0:T(8,128)} %get-tuple-element.10.own_ref), channel_id=1, source_target_pairs={{0,1},{1,2},{2,3},{3,4},{4,5},{5,6},{6,7},{7,64},{64,65},{65,66},{... | collective-permute-start | bytes 98312 | tf_op jit(solution)/shard_map/ppermute | solution.py:549
  5.8 4.0 %all-to-all-start = ((f32[4,1,26624]{2,1,0:T(1,128)}), f32[4,1,26624]{2,1,0:T(1,128)S(1)}, u32[]{:S(2)}, u32[]{:S(2)}) async-start(f32[4,1,26624]{2,1,0:T(1,128)} %bitcast.37), calls=%async_computation | async-start | bytes 851968 | tf_op jit(solution)/shard_map/all_to_all | solution.py:500
  9.8 0.0 collective-permute-done.near_ref
  9.8 0.0 copy-done.5
  9.8 0.0 copy-start.3
  9.8 0.7 copy-done.3
  10.5 4.3 %spread.1 = f32[2048,128]{1,0:T(8,128)} custom-call(f32[8,1024]{1,0:T(8,128)S(1)} %copy-done.3, f32[8,1024]{1,0:T(8,128)S(1)} %collective-permute-done.near_ref, bf16[384,960]{1,0:T(8,128)(2,1)S(1)} %copy-done.5), custom_call_target="tpu_custom_call" | custom-call | flops 40000000000 | bytes 10000000 | tf_op jit(solution)/shard_map/spread/pallas_call | solution.py:551
  14.8 3.8 %all-to-all-done = f32[4,1,26624]{2,1,0:T(1,128)S(1)} async-done(((f32[4,1,26624]{2,1,0:T(1,128)}), f32[4,1,26624]{2,1,0:T(1,128)S(1)}, u32[]{:S(2)}, u32[]{:S(2)}) %all-to-all-start) | async-done | bytes 426016 | tf_op jit(solution)/shard_map/all_to_all | solution.py:500
  18.7 7.9 %collective-permute-start.1 = (f32[4,104,128]{2,1,0:T(8,128)S(1)}, f32[4,104,128]{2,1,0:T(8,128)S(1)}, u32[]{:S(2)}, u32[]{:S(2)}) collective-permute-start(f32[4,104,128]{2,1,0:T(8,128)S(1)} %dynamic-slice_bitcast_fusion), channel_id=1, source_target_pairs={{0,8},{8,0},{16,24},{24,16},{32,40},{40,32},{1,9},{9,1},{17,25},{2... | collective-permute-start | bytes 638984 | tf_op jit(solution)/shard_map/ppermute | solution.py:513
  26.6 7.0 %all-to-all-start.1 = ((f32[256,1,1024]{2,1,0:T(1,128)}), f32[256,1,1024]{2,1,0:T(1,128)S(1)}, u32[]{:S(2)}, u32[]{:S(2)}) async-start(f32[256,1,1024]{2,1,0:T(1,128)} %bitcast.3), calls=%async_computation.1 | async-start | bytes 2097152 | tf_op jit(solution)/shard_map/all_to_all | solution.py:494
  33.6 0.0 collective-permute-done.1
  33.7 0.1 fusion.3
  33.9 0.5 reshape.43
  34.4 1.3 %copy.20 = f32[32,40,10,8]{1,0,3,2:T(8,128)} copy(f32[32,40,10,8]{1,3,0,2:T(8,128)S(1)} %bitcast.32) | data formatting | bytes 819200 | tf_op jit(solution)/shard_map/transpose | solution.py:519
  35.7 2.0 %reshape.44 = f32[1280,80]{0,1:T(8,128)S(1)} reshape(f32[32,40,10,8]{1,0,3,2:T(8,128)} %copy.20) | data formatting | bytes 819200 | tf_op jit(solution)/shard_map/reshape | solution.py:519
  37.7 0.2 copy.21.in_ref
  38.0 0.0 copy-start.1
  38.0 0.0 copy-start.2
  38.0 0.1 widen.1.influence_ref
  38.1 28.0 %all-to-all-done.1 = f32[256,1,1024]{2,1,0:T(1,128)S(1)} async-done(((f32[256,1,1024]{2,1,0:T(1,128)}), f32[256,1,1024]{2,1,0:T(1,128)S(1)}, u32[]{:S(2)}, u32[]{:S(2)}) %all-to-all-start.1) | async-done | bytes 1048608 | tf_op jit(solution)/shard_map/all_to_all | solution.py:494
  66.1 0.0 copy-done.1
  66.1 0.0 copy-done.2
  66.1 4.6 %plane.1 = f32[2048,128]{1,0:T(8,128)S(1)} custom-call(f32[2048,128]{1,0:T(8,128)S(1)} %bitcast.29, f32[1280,128]{1,0:T(8,128)S(1)} %widen.1.influence_ref, bf16[1056,256]{1,0:T(8,128)(2,1)S(1)} %copy-done.1, f32[336,128]{1,0:T(8,128)S(1)} %copy-done.2), custom_call_target="tpu_custom_call" | custom-call | tf_op jit(solution)/shard_map/plane/pallas_call | solution.py:562
  70.7 0.0 copy-start
  70.7 38.5 %all_to_all.15 = f32[256,1,1024]{2,1,0:T(1,128)S(1)} all-to-all(f32[256,1,1024]{2,1,0:T(1,128)S(1)} %bitcast.30), channel_id=1, replica_groups=mesh['gx'=4,'gy'=8,'gz'=8] {'gx','gy','gz'}, dimensions={0} | all-to-all | bytes 2097152 | tf_op jit(solution)/shard_map/all_to_all | solution.py:494
  109.2 0.0 copy-start.4
  109.2 0.0 copy-done
  109.2 2.8 %near.1 = (bf16[480,1024]{1,0:T(8,128)(2,1)S(1)}, f32[4,1024]{1,0:T(4,128)S(1)}) custom-call(f32[2048,128]{1,0:T(8,128)S(1)} %bitcast.31, f32[8,1024]{1,0:T(8,128)S(1)} %collective-permute-done.near_ref, bf16[384,1152]{1,0:T(8,128)(2,1)S(1)} %copy-done), custom_call_target="tpu_custom_call" | custom-call | tf_op jit(solution)/shard_map/near/pallas_call | solution.py:575
  112.0 0.1 collective-permute-start.2
  112.1 0.0 copy-done.4
  112.1 2.6 %own.1.inner_ref = f32[4,1024]{1,0:T(4,128)S(1)} custom-call(bf16[480,1024]{1,0:T(8,128)(2,1)S(1)} %get-tuple-element.15.mesh_ref, f32[8,1024]{1,0:T(8,128)S(1)} %copy-done.4), custom_call_target="tpu_custom_call" | custom-call | tf_op jit(solution)/shard_map/own/pallas_call | solution.py:583
  114.7 0.5 collective-permute-done.2.edge_ref
  115.2 0.6 finish.1
  (5 shorter events, 0.1 us)
Async XLA Ops:
  0.6 9.1 %copy-start.5 = (bf16[384,960]{1,0:T(8,128)(2,1)S(1)}, bf16[384,960]{1,0:T(8,128)(2,1)}, u32[]{:S(2)}) copy-start(bf16[384,960]{1,0:T(8,128)(2,1)} %constant.36.clone.front_ref) | copy-start | bytes 2211844
  2.7 7.1 %collective-permute-start = (f32[8,1024]{1,0:T(8,128)}, f32[8,1024]{1,0:T(8,128)S(1)}, u32[]{:S(2)}, u32[]{:S(2)}) collective-permute-start(f32[8,1024]{1,0:T(8,128)} %get-tuple-element.10.own_ref), channel_id=1, source_target_pairs={{0,1},{1,2},{2,3},{3,4},{4,5},{5,6},{6,7},{7,64},{64,65},{65,66},{... | collective-permute-start | bytes 98312 | tf_op jit(solution)/shard_map/ppermute | solution.py:549
  5.8 12.9 %all-to-all-start = ((f32[4,1,26624]{2,1,0:T(1,128)}), f32[4,1,26624]{2,1,0:T(1,128)S(1)}, u32[]{:S(2)}, u32[]{:S(2)}) async-start(f32[4,1,26624]{2,1,0:T(1,128)} %bitcast.37), calls=%async_computation | async-start | bytes 851968 | tf_op jit(solution)/shard_map/all_to_all | solution.py:500
  9.8 0.8 copy-start.3
  18.7 15.0 %collective-permute-start.1 = (f32[4,104,128]{2,1,0:T(8,128)S(1)}, f32[4,104,128]{2,1,0:T(8,128)S(1)}, u32[]{:S(2)}, u32[]{:S(2)}) collective-permute-start(f32[4,104,128]{2,1,0:T(8,128)S(1)} %dynamic-slice_bitcast_fusion), channel_id=1, source_target_pairs={{0,8},{8,0},{16,24},{24,16},{32,40},{40,32},{1,9},{9,1},{17,25},{2... | collective-permute-start | bytes 638984 | tf_op jit(solution)/shard_map/ppermute | solution.py:513
  26.6 39.5 %all-to-all-start.1 = ((f32[256,1,1024]{2,1,0:T(1,128)}), f32[256,1,1024]{2,1,0:T(1,128)S(1)}, u32[]{:S(2)}, u32[]{:S(2)}) async-start(f32[256,1,1024]{2,1,0:T(1,128)} %bitcast.3), calls=%async_computation.1 | async-start | bytes 2097152 | tf_op jit(solution)/shard_map/all_to_all | solution.py:494
  38.0 28.1 %copy-start.1 = (bf16[1056,256]{1,0:T(8,128)(2,1)S(1)}, bf16[1056,256]{1,0:T(8,128)(2,1)}, u32[]{:S(2)}) copy-start(bf16[1056,256]{1,0:T(8,128)(2,1)} %constant.38.clone.mixes_ref) | copy-start | bytes 1622020
  38.0 28.1 %copy-start.2 = (f32[336,128]{1,0:T(8,128)S(1)}, f32[336,128]{1,0:T(8,128)}, u32[]{:S(2)}) copy-start(f32[336,128]{1,0:T(8,128)} %constant.39.clone.turns_ref) | copy-start | bytes 516100
  70.7 38.5 %copy-start = (bf16[384,1152]{1,0:T(8,128)(2,1)S(1)}, bf16[384,1152]{1,0:T(8,128)(2,1)}, u32[]{:S(2)}) copy-start(bf16[384,1152]{1,0:T(8,128)(2,1)} %constant.37.clone.back_ref) | copy-start | bytes 2654212
  109.2 2.9 %copy-start.4 = (f32[8,1024]{1,0:T(8,128)S(1)}, f32[8,1024]{1,0:T(8,128)}, u32[]{:S(2)}) copy-start(f32[8,1024]{1,0:T(8,128)} %get-tuple-element.10.own_ref) | copy-start | bytes 98308
  112.0 3.2 %collective-permute-start.2 = (f32[4,1024]{1,0:T(4,128)S(1)}, f32[4,1024]{1,0:T(4,128)S(1)}, u32[]{:S(2)}, u32[]{:S(2)}) collective-permute-start(f32[4,1024]{1,0:T(4,128)S(1)} %get-tuple-element.14), channel_id=1, source_target_pairs={{0,199},{1,0},{2,1},{3,2},{4,3},{5,4},{6,5},{7,6},{64,7},{65,64},{... | collective-permute-start | bytes 49160 | tf_op jit(solution)/shard_map/ppermute | solution.py:582

commit v2 on v1

--- a/solution.py
+++ b/solution.py
@@ -439,12 +439,13 @@
             for x in range(columns):
                 row = (g * columns + x) * STEP_Y
                 value = near[row : row + STEP_Y]
-                weighted = wy * value
-                wx = weight_x[x : x + 1, lanes]
-                sums[0] = sums[0] + wx * weighted
-                sums[1] = sums[1] + slope_x[x : x + 1, lanes] * weighted
-                sums[2] = sums[2] + wx * (sy * value)
-                sums[3] = sums[3] + wx * (wy * near_slope[row : row + STEP_Y])
+                weight, slope = weight_x[x : x + 1, lanes], slope_x[x : x + 1, lanes]
+                terms = [weight * value, slope * value, weight * near_slope[row : row + STEP_Y]]
+                along = terms if x == 0 else [total + term for total, term in zip(along, terms)]
+            sums[0] = sums[0] + wy * along[0]
+            sums[1] = sums[1] + wy * along[1]
+            sums[2] = sums[2] + sy * along[0]
+            sums[3] = sums[3] + wy * along[2]
         finish(lanes, [jnp.sum(part, axis=0, keepdims=True) for part in sums])
 
 

time: 116 us -> 116 us (level)
  no operation moved by 1% of the time
where the time goes in v2:
time: 116 us
  blocking collectives  38.5 us (33%)
  waiting for transfers between devices  32.4 us (28%)
  starting transfers between devices  22.1 us (19%)
  Pallas kernels  16.8 us (14%)
  local copies, waits for them, and re-layouts  4.96 us (4%)
    all_to_all x1, blocking collectives, exchange(): lax.all_to_all(flat, ('gx', 'gy', 'gz'), 0, 0, tiled=True)  38.5 us
    all_to_all x1, waiting for transfers between devices, exchange(): lax.all_to_all(flat, ('gx', 'gy', 'gz'), 0, 0, tiled=True)  28 us
    ppermute x1, starting transfers between devices, influence_layout(): other = lax.ppermute(sent, 'gy', [(s, s ^ 1) for s in range(SLOTS)])  7.9 us
    all_to_all x1, starting transfers between devices, exchange(): lax.all_to_all(flat, ('gx', 'gy', 'gz'), 0, 0, tiled=True)  7.05 us
    pallas_call x1, Pallas kernels, body(): pl.pallas_call(plane_kernel, out_shape=jax.ShapeDtypeStruct((ROWS, LANES)...  4.59 us
    pallas_call x1, Pallas kernels, body(): pl.pallas_call(spread_kernel, out_shape=jax.ShapeDtypeStruct((ROWS, LANES...  4.28 us
    all_to_all x1, starting transfers between devices, influence_along_x(): lax.all_to_all(flat, 'gy', 0, 0, tiled=True, axis_index_groups=groups)  4.01 us
    all_to_all x1, waiting for transfers between devices, influence_along_x(): lax.all_to_all(flat, 'gy', 0, 0, tiled=True, axis_index_groups=groups)  3.81 us
  transfers between devices with their start and end apart: 5, of which 3 were waited for; matrix products, arithmetic and copies ran while one was open for 4% of the time, Pallas kernels for 6%

profile of v2, /device:TPU:1, one launch (start us, length us, event | category | flops | bytes accessed | tf_op | source)
XLA Modules:
  0.0 115.8 jit_solution(17048976323124429360)
XLA Ops:
  0.6 0.0 copy-start.5
  0.6 2.0 %pack.1 = (f32[8,1024]{1,0:T(8,128)}, f32[832,128]{1,0:T(8,128)}) custom-call(f32[1,1024]{1,0:T(1,128)} %bitcast.38, s32[3,1024]{1,0:T(4,128)} %start_in.1, f32[3,1024]{1,0:T(4,128)} %frac_in.1, f32[10,40,320]{2,1,0:T(8,128)} %influence_in.1), custom_call_target="tpu_custom_call" | custom-call | tf_op jit(solution)/shard_map/pack/pallas_call | solution.py:533
  2.7 3.1 %collective-permute-start = (f32[8,1024]{1,0:T(8,128)}, f32[8,1024]{1,0:T(8,128)S(1)}, u32[]{:S(2)}, u32[]{:S(2)}) collective-permute-start(f32[8,1024]{1,0:T(8,128)} %get-tuple-element.10.own_ref), channel_id=1, source_target_pairs={{0,1},{1,2},{2,3},{3,4},{4,5},{5,6},{6,7},{7,64},{64,65},{65,66},{... | collective-permute-start | bytes 98312 | tf_op jit(solution)/shard_map/ppermute | solution.py:550
  5.8 4.0 %all-to-all-start = ((f32[4,1,26624]{2,1,0:T(1,128)}), f32[4,1,26624]{2,1,0:T(1,128)S(1)}, u32[]{:S(2)}, u32[]{:S(2)}) async-start(f32[4,1,26624]{2,1,0:T(1,128)} %bitcast.37), calls=%async_computation | async-start | bytes 851968 | tf_op jit(solution)/shard_map/all_to_all | solution.py:501
  9.8 0.0 collective-permute-done.near_ref
  9.8 0.0 copy-done.5
  9.8 0.0 copy-start.3
  9.8 0.7 copy-done.3
  10.5 4.3 %spread.1 = f32[2048,128]{1,0:T(8,128)} custom-call(f32[8,1024]{1,0:T(8,128)S(1)} %copy-done.3, f32[8,1024]{1,0:T(8,128)S(1)} %collective-permute-done.near_ref, bf16[384,960]{1,0:T(8,128)(2,1)S(1)} %copy-done.5), custom_call_target="tpu_custom_call" | custom-call | flops 40000000000 | bytes 10000000 | tf_op jit(solution)/shard_map/spread/pallas_call | solution.py:552
  14.8 3.8 %all-to-all-done = f32[4,1,26624]{2,1,0:T(1,128)S(1)} async-done(((f32[4,1,26624]{2,1,0:T(1,128)}), f32[4,1,26624]{2,1,0:T(1,128)S(1)}, u32[]{:S(2)}, u32[]{:S(2)}) %all-to-all-start) | async-done | bytes 426016 | tf_op jit(solution)/shard_map/all_to_all | solution.py:501
  18.7 7.9 %collective-permute-start.1 = (f32[4,104,128]{2,1,0:T(8,128)S(1)}, f32[4,104,128]{2,1,0:T(8,128)S(1)}, u32[]{:S(2)}, u32[]{:S(2)}) collective-permute-start(f32[4,104,128]{2,1,0:T(8,128)S(1)} %dynamic-slice_bitcast_fusion), channel_id=1, source_target_pairs={{0,8},{8,0},{16,24},{24,16},{32,40},{40,32},{1,9},{9,1},{17,25},{2... | collective-permute-start | bytes 638984 | tf_op jit(solution)/shard_map/ppermute | solution.py:514
  26.6 7.0 %all-to-all-start.1 = ((f32[256,1,1024]{2,1,0:T(1,128)}), f32[256,1,1024]{2,1,0:T(1,128)S(1)}, u32[]{:S(2)}, u32[]{:S(2)}) async-start(f32[256,1,1024]{2,1,0:T(1,128)} %bitcast.3), calls=%async_computation.1 | async-start | bytes 2097152 | tf_op jit(solution)/shard_map/all_to_all | solution.py:495
  33.6 0.0 collective-permute-done.1
  33.7 0.1 fusion.3
  33.9 0.5 reshape.43
  34.4 1.3 %copy.20 = f32[32,40,10,8]{1,0,3,2:T(8,128)} copy(f32[32,40,10,8]{1,3,0,2:T(8,128)S(1)} %bitcast.32) | data formatting | bytes 819200 | tf_op jit(solution)/shard_map/transpose | solution.py:520
  35.7 2.0 %reshape.44 = f32[1280,80]{0,1:T(8,128)S(1)} reshape(f32[32,40,10,8]{1,0,3,2:T(8,128)} %copy.20) | data formatting | bytes 819200 | tf_op jit(solution)/shard_map/reshape | solution.py:520
  37.7 0.2 copy.21.in_ref
  38.0 0.0 copy-start.1
  38.0 0.0 copy-start.2
  38.0 0.1 widen.1.influence_ref
  38.1 28.0 %all-to-all-done.1 = f32[256,1,1024]{2,1,0:T(1,128)S(1)} async-done(((f32[256,1,1024]{2,1,0:T(1,128)}), f32[256,1,1024]{2,1,0:T(1,128)S(1)}, u32[]{:S(2)}, u32[]{:S(2)}) %all-to-all-start.1) | async-done | bytes 1048608 | tf_op jit(solution)/shard_map/all_to_all | solution.py:495
  66.1 0.0 copy-done.1
  66.1 0.0 copy-done.2
  66.1 4.6 %plane.1 = f32[2048,128]{1,0:T(8,128)S(1)} custom-call(f32[2048,128]{1,0:T(8,128)S(1)} %bitcast.29, f32[1280,128]{1,0:T(8,128)S(1)} %widen.1.influence_ref, bf16[1056,256]{1,0:T(8,128)(2,1)S(1)} %copy-done.1, f32[336,128]{1,0:T(8,128)S(1)} %copy-done.2), custom_call_target="tpu_custom_call" | custom-call | tf_op jit(solution)/shard_map/plane/pallas_call | solution.py:563
  70.7 0.0 copy-start
  70.7 38.5 %all_to_all.15 = f32[256,1,1024]{2,1,0:T(1,128)S(1)} all-to-all(f32[256,1,1024]{2,1,0:T(1,128)S(1)} %bitcast.30), channel_id=1, replica_groups=mesh['gx'=4,'gy'=8,'gz'=8] {'gx','gy','gz'}, dimensions={0} | all-to-all | bytes 2097152 | tf_op jit(solution)/shard_map/all_to_all | solution.py:495
  109.2 0.0 copy-start.4
  109.2 0.0 copy-done
  109.2 2.7 %near.1 = (bf16[480,1024]{1,0:T(8,128)(2,1)S(1)}, f32[4,1024]{1,0:T(4,128)S(1)}) custom-call(f32[2048,128]{1,0:T(8,128)S(1)} %bitcast.31, f32[8,1024]{1,0:T(8,128)S(1)} %collective-permute-done.near_ref, bf16[384,1152]{1,0:T(8,128)(2,1)S(1)} %copy-done), custom_call_target="tpu_custom_call" | custom-call | tf_op jit(solution)/shard_map/near/pallas_call | solution.py:576
  111.9 0.1 collective-permute-start.2
  112.0 0.0 copy-done.4
  112.0 2.5 %own.1.inner_ref = f32[4,1024]{1,0:T(4,128)S(1)} custom-call(bf16[480,1024]{1,0:T(8,128)(2,1)S(1)} %get-tuple-element.15.mesh_ref, f32[8,1024]{1,0:T(8,128)S(1)} %copy-done.4), custom_call_target="tpu_custom_call" | custom-call | tf_op jit(solution)/shard_map/own/pallas_call | solution.py:584
  114.5 0.6 collective-permute-done.2.edge_ref
  115.1 0.6 finish.1
  (5 shorter events, 0.1 us)
Async XLA Ops:
  0.6 9.1 %copy-start.5 = (bf16[384,960]{1,0:T(8,128)(2,1)S(1)}, bf16[384,960]{1,0:T(8,128)(2,1)}, u32[]{:S(2)}) copy-start(bf16[384,960]{1,0:T(8,128)(2,1)} %constant.36.clone.front_ref) | copy-start | bytes 2211844
  2.7 7.1 %collective-permute-start = (f32[8,1024]{1,0:T(8,128)}, f32[8,1024]{1,0:T(8,128)S(1)}, u32[]{:S(2)}, u32[]{:S(2)}) collective-permute-start(f32[8,1024]{1,0:T(8,128)} %get-tuple-element.10.own_ref), channel_id=1, source_target_pairs={{0,1},{1,2},{2,3},{3,4},{4,5},{5,6},{6,7},{7,64},{64,65},{65,66},{... | collective-permute-start | bytes 98312 | tf_op jit(solution)/shard_map/ppermute | solution.py:550
  5.8 12.9 %all-to-all-start = ((f32[4,1,26624]{2,1,0:T(1,128)}), f32[4,1,26624]{2,1,0:T(1,128)S(1)}, u32[]{:S(2)}, u32[]{:S(2)}) async-start(f32[4,1,26624]{2,1,0:T(1,128)} %bitcast.37), calls=%async_computation | async-start | bytes 851968 | tf_op jit(solution)/shard_map/all_to_all | solution.py:501
  9.8 0.8 copy-start.3
  18.7 15.0 %collective-permute-start.1 = (f32[4,104,128]{2,1,0:T(8,128)S(1)}, f32[4,104,128]{2,1,0:T(8,128)S(1)}, u32[]{:S(2)}, u32[]{:S(2)}) collective-permute-start(f32[4,104,128]{2,1,0:T(8,128)S(1)} %dynamic-slice_bitcast_fusion), channel_id=1, source_target_pairs={{0,8},{8,0},{16,24},{24,16},{32,40},{40,32},{1,9},{9,1},{17,25},{2... | collective-permute-start | bytes 638984 | tf_op jit(solution)/shard_map/ppermute | solution.py:514
  26.6 39.5 %all-to-all-start.1 = ((f32[256,1,1024]{2,1,0:T(1,128)}), f32[256,1,1024]{2,1,0:T(1,128)S(1)}, u32[]{:S(2)}, u32[]{:S(2)}) async-start(f32[256,1,1024]{2,1,0:T(1,128)} %bitcast.3), calls=%async_computation.1 | async-start | bytes 2097152 | tf_op jit(solution)/shard_map/all_to_all | solution.py:495
  38.0 28.1 %copy-start.1 = (bf16[1056,256]{1,0:T(8,128)(2,1)S(1)}, bf16[1056,256]{1,0:T(8,128)(2,1)}, u32[]{:S(2)}) copy-start(bf16[1056,256]{1,0:T(8,128)(2,1)} %constant.38.clone.mixes_ref) | copy-start | bytes 1622020
  38.0 28.1 %copy-start.2 = (f32[336,128]{1,0:T(8,128)S(1)}, f32[336,128]{1,0:T(8,128)}, u32[]{:S(2)}) copy-start(f32[336,128]{1,0:T(8,128)} %constant.39.clone.turns_ref) | copy-start | bytes 516100
  70.7 38.5 %copy-start = (bf16[384,1152]{1,0:T(8,128)(2,1)S(1)}, bf16[384,1152]{1,0:T(8,128)(2,1)}, u32[]{:S(2)}) copy-start(bf16[384,1152]{1,0:T(8,128)(2,1)} %constant.37.clone.back_ref) | copy-start | bytes 2654212
  109.2 2.8 %copy-start.4 = (f32[8,1024]{1,0:T(8,128)S(1)}, f32[8,1024]{1,0:T(8,128)}, u32[]{:S(2)}) copy-start(f32[8,1024]{1,0:T(8,128)} %get-tuple-element.10.own_ref) | copy-start | bytes 98308
  111.9 3.2 %collective-permute-start.2 = (f32[4,1024]{1,0:T(4,128)S(1)}, f32[4,1024]{1,0:T(4,128)S(1)}, u32[]{:S(2)}, u32[]{:S(2)}) collective-permute-start(f32[4,1024]{1,0:T(4,128)S(1)} %get-tuple-element.14), channel_id=1, source_target_pairs={{0,199},{1,0},{2,1},{3,2},{4,3},{5,4},{6,5},{7,6},{64,7},{65,64},{... | collective-permute-start | bytes 49160 | tf_op jit(solution)/shard_map/ppermute | solution.py:583
